TPU v7x, 256 devices: a whole 4x4x8 slice. The times are simulated.
256 devices in a mesh: tile: 128 (over y, x, z), chol: 2 (over core).
Axes of the slice: x: 4, y: 4, z: 8, core: 2. Of those that a mesh axis runs over, the one named last changes fastest.
Arguments:
- amplitudes: bfloat16 [120, 2, 1024, 1024], P('chol', None, 'tile'), may hold values from -6 to 6
- cholesky: bfloat16 [120, 1024, 896], P(None, 'tile', 'chol'), may hold values from -0.0625 to 0.0625
Outputs:
- cycle_term: bfloat16 [120, 2, 1024, 1024], P('chol', None, 'tile')
All inputs are finite; a program needn't handle non-finite values.
Results may differ from a plain program's by a relative error of at most 0.0049.
Values may be sent and summed in bfloat16 or wider, within the bound.
A program may use at most 64 MiB of HBM per device.

v0:
```python
import jax
import jax.numpy as jnp
from jax import lax
from jax.sharding import PartitionSpec as P


def shards(amplitudes, cholesky):
    all_vectors = lax.all_gather(cholesky, "chol", axis=2, tiled=True)
    own_rows = amplitudes.shape[0]
    own_vectors = lax.dynamic_slice_in_dim(
        all_vectors, lax.axis_index("chol") * own_rows, own_rows, 0
    )
    partial_term = jnp.einsum(
        "kjbc,kcp->bjp",
        lax.all_to_all(amplitudes, "tile", split_axis=3, concat_axis=2, tiled=True),
        own_vectors,
        preferred_element_type=jnp.float32,
    )
    shared_rows = lax.psum_scatter(
        partial_term, ("tile", "chol"), scatter_dimension=0, tiled=True
    ).astype(jnp.bfloat16)
    product = jnp.einsum(
        "bjp,iap->ijba",
        lax.all_gather(shared_rows, ("tile", "chol"), axis=0, tiled=True),
        own_vectors,
        preferred_element_type=jnp.float32,
    )
    local_cycle = product.astype(jnp.bfloat16)
    return lax.all_to_all(local_cycle, "tile", split_axis=2, concat_axis=3, tiled=True)


def solution(mesh):
    in_specs = (P("chol", None, "tile", None), P(None, "tile", "chol"))
    out_specs = P("chol", None, "tile", None)
    return jax.shard_map(shards, mesh=mesh, in_specs=in_specs, out_specs=out_specs, check_vma=False)
```

profile of v0, /device:TPU:1, one launch (start us, length us, event | category | flops | bytes accessed | tf_op | source)
XLA Modules:
  0.0 504.3 jit_solution(14919378088592587701)
XLA Ops:
  6.5 7.2 %copy.26 = bf16[60,2,8,1024]{0,2,1,3:T(8,128)(2,1)} copy(bf16[60,2,8,1024]{3,2,1,0:T(8,128)(2,1)} %param.2) | data formatting | bytes 3932160 | tf_op args[0]
  13.7 14.6 %reshape.5 = bf16[128,2,3840]{2,1,0:T(2,128)(2,1)} reshape(bf16[1024,2,8,60]{3,2,1,0:T(8,128)(2,1)} %bitcast.35) | data formatting | bytes 3932160
  28.3 16.3 %all-to-all-start = ((bf16[128,2,3840]{2,1,0:T(2,128)(2,1)}), bf16[128,2,3840]{2,1,0:T(2,128)(2,1)S(1)}, u32[]{:S(2)}, u32[]{:S(2)}) async-start(bf16[128,2,3840]{2,1,0:T(2,128)(2,1)} %reshape.5), calls=%async_computation | async-start | bytes 3932160 | tf_op jit(solution)/shard_map/all_to_all | solution.py:15
  44.7 1.5 copy.24
  46.5 18.3 %all-gather.3.cloned.1.call-done = bf16[120,8,896]{0,1,2:T(8,128)(2,1)} async-done(((bf16[120,8,448]{0,1,2:T(8,128)(2,1)}), bf16[120,8,896]{0,1,2:T(8,128)(2,1)}) %all-gather.3.cloned.1.call-update) | async-done | bytes 1720336 | tf_op jit(solution)/shard_map/all_gather | solution.py:8
  64.8 3.3 constant_dynamic-slice_fusion
  68.1 3.7 copy.43
  71.8 22.7 %all-to-all-done = bf16[128,2,3840]{2,1,0:T(2,128)(2,1)S(1)} async-done(((bf16[128,2,3840]{2,1,0:T(2,128)(2,1)}), bf16[128,2,3840]{2,1,0:T(2,128)(2,1)S(1)}, u32[]{:S(2)}, u32[]{:S(2)}) %all-to-all-start) | async-done | bytes 1966112 | tf_op jit(solution)/shard_map/all_to_all | solution.py:15
  94.5 15.2 %reshape.6 = bf16[1024,2,8,60]{3,2,1,0:T(8,128)(2,1)} reshape(bf16[128,2,3840]{2,1,0:T(2,128)(2,1)S(1)} %all-to-all-done) | data formatting | bytes 3932160
  109.7 5.8 %copy.28 = bf16[60,2,128,8,8]{0,4,3,2,1:T(8,128)(2,1)} copy(bf16[60,2,128,8,8]{0,3,1,4,2:T(8,128)(2,1)} %bitcast.36) | data formatting | bytes 3932160 | tf_op jit(solution)/shard_map/all_to_all | solution.py:15
  115.5 6.0 %copy.29 = bf16[60,2,1024,8]{2,3,0,1:T(8,128)(2,1)S(1)} copy(bf16[60,2,1024,8]{0,3,2,1:T(8,128)(2,1)} %bitcast.37) | data formatting | bytes 3932160 | tf_op jit(solution)/shard_map/all_to_all | solution.py:15
  121.5 5.1 %convolution_bitcast_fusion = f32[1024,2,896]{0,2,1:T(8,128)} fusion(bf16[60,2,1024,8]{2,3,0,1:T(8,128)(2,1)S(1)} %copy.29, bf16[60,8,896]{2,1,0:T(8,128)(2,1)S(1)} %copy.43), kind=kOutput, calls=%fused_computation.4 | convolution fusion | flops 1761607680 | bytes 10166272 | tf_op jit(solution)/shard_map/kjbc,kcp->bjp/dot_general | solution.py:13
  126.6 8.1 %copy.30 = f32[1024,2,896]{2,0,1:T(8,128)} copy(f32[1024,2,896]{0,2,1:T(8,128)} %convolution_bitcast_fusion) | data formatting | bytes 14680064 | tf_op jit(solution)/shard_map/kjbc,kcp->bjp/transpose | solution.py:13
  134.7 138.4 %all-reduce.2 = bf16[1024,2,896]{2,0,1:T(8,128)(2,1)} all-reduce(f32[1024,2,896]{2,0,1:T(8,128)} %copy.30), channel_id=2, replica_groups=mesh['tile'=128,'chol'=2] {'tile','chol'}, use_global_device_ids=true, to_apply=%region_0.0.clone | all-reduce | flops 1835008 | bytes 11010048
  273.1 0.8 dynamic-slice_convert_fusion
  273.8 0.6 copy.31
  274.5 111.3 %all-gather.5.cloned.1.call-done = bf16[1024,2,896]{2,1,0:T(2,128)(2,1)} async-done(((bf16[4,2,896]{2,1,0:T(2,128)(2,1)}), bf16[1024,2,896]{2,1,0:T(2,128)(2,1)}) %all-gather.5.cloned.1.call-update) | async-done | bytes 3670032 | tf_op jit(solution)/shard_map/all_gather | solution.py:24
  385.8 4.3 convert_bitcast_fusion
  390.1 6.2 %copy.33 = bf16[60,2,1024,8]{0,3,1,2:T(8,128)(2,1)} copy(bf16[60,2,1024,8]{2,3,1,0:T(8,128)(2,1)S(1)} %convert_bitcast_fusion) | data formatting | bytes 3932160 | tf_op jit(solution)/shard_map/convert_element_type | solution.py:28
  396.3 13.8 %reshape.7 = bf16[128,2,3840]{2,1,0:T(2,128)(2,1)S(1)} reshape(bf16[1024,2,8,60]{3,2,1,0:T(8,128)(2,1)} %bitcast.34) | data formatting | bytes 3932160
  410.1 60.2 %all_to_all.36 = bf16[128,2,3840]{2,1,0:T(2,128)(2,1)} all-to-all(bf16[128,2,3840]{2,1,0:T(2,128)(2,1)S(1)} %reshape.7), channel_id=1, replica_groups=mesh['tile'=128,'chol'=2] {'tile'}, dimensions={0} | all-to-all | bytes 3932160 | tf_op jit(solution)/shard_map/all_to_all | solution.py:29
  470.4 16.0 %reshape.8 = bf16[1024,2,8,60]{3,2,1,0:T(8,128)(2,1)} reshape(bf16[128,2,3840]{2,1,0:T(2,128)(2,1)} %all_to_all.36) | data formatting | bytes 3932160
  486.4 5.2 %copy.51 = bf16[60,2,8,128,8]{0,4,3,2,1:T(8,128)(2,1)} copy(bf16[60,2,8,128,8]{0,4,1,2,3:T(8,128)(2,1)} %bitcast.38) | data formatting | bytes 3932160 | tf_op jit(solution)/shard_map/all_to_all | solution.py:29
  491.6 5.8 %copy.36 = bf16[60,2,8,1024]{3,2,1,0:T(8,128)(2,1)} copy(bf16[60,2,8,1024]{0,3,2,1:T(8,128)(2,1)} %bitcast.39) | data formatting | bytes 3932160 | tf_op jit(solution)/shard_map/all_to_all | solution.py:29
  (6 shorter events, 0.3 us)
Async XLA Ops:
  13.7 30.9 %copy-start = (bf16[120,8,448]{0,2,1:T(8,128)(2,1)S(1)}, bf16[120,8,448]{0,2,1:T(8,128)(2,1)}, u32[]{:S(2)}) copy-start(bf16[120,8,448]{0,2,1:T(8,128)(2,1)} %param.3) | copy-start | bytes 2580484
  28.3 66.3 %all-to-all-start = ((bf16[128,2,3840]{2,1,0:T(2,128)(2,1)}), bf16[128,2,3840]{2,1,0:T(2,128)(2,1)S(1)}, u32[]{:S(2)}, u32[]{:S(2)}) async-start(bf16[128,2,3840]{2,1,0:T(2,128)(2,1)} %reshape.5), calls=%async_computation | async-start | bytes 3932160 | tf_op jit(solution)/shard_map/all_to_all | solution.py:15
  44.6 20.2 %all-gather.3.cloned.1.call-start = ((), (), s32[]{:S(2)}) async-start(), calls=%async_computation.2 | async-start | bytes 2752512 | tf_op jit(solution)/shard_map/all_gather | solution.py:8
  46.2 339.6 %all-gather.5.cloned.1.call-start = ((), (), s32[]{:S(2)}) async-start(), calls=%async_computation.3 | async-start | bytes 3684352 | tf_op jit(solution)/shard_map/all_gather | solution.py:24
Sparse Core Ops, SparseCore 0:
  47.2 17.5 all-gather.2
  274.6 111.1 all-gather.4
where the time goes:
time: 505 us; the launch traced here: 504 us
  blocking collectives  199 us (39%)
  waiting for transfers between devices  152 us (30%)
  local copies, waits for them, and re-layouts  114 us (23%)
  starting transfers between devices  16.6 us (3%)
  between operations  13.5 us (3%)
  matrix products  9.4 us (2%)
    unnamed x1, blocking collectives  138 us
    all_gather x1, waiting for transfers between devices, shards(): lax.all_gather(shared_rows, ('tile', 'chol'), axis=0, tiled=True)  111 us
    unnamed x9, local copies, waits for them, and re-layouts  72 us
    all_to_all x1, blocking collectives, shards(): lax.all_to_all(local_cycle, 'tile', split_axis=2, concat_axis=3, tiled=True)  60.2 us
    all_to_all x1, waiting for transfers between devices, shards(): lax.all_to_all(amplitudes, 'tile', split_axis=3, concat_axis=2, tiled=True)  22.7 us
    all_gather x1, waiting for transfers between devices, shards(): all_vectors = lax.all_gather(cholesky, 'chol', axis=2, tiled=True)  18.3 us
    all_to_all x1, starting transfers between devices, shards(): lax.all_to_all(amplitudes, 'tile', split_axis=3, concat_axis=2, tiled=True)  16.3 us
    all_to_all x2, local copies, waits for them, and re-layouts, shards(): lax.all_to_all(amplitudes, 'tile', split_axis=3, concat_axis=2, tiled=True)  11.8 us
  transfers between devices with their start and end apart: 3, of which 3 were waited for; matrix products, arithmetic and copies ran while one was open for 2% of the time, Pallas kernels for 0%

commit v1 on v0

v1 whole, which is shorter than its diff:
```python
import functools

import jax
import jax.numpy as jnp
from jax import lax
from jax.experimental import pallas as pl
from jax.experimental.pallas import tpu as pltpu
from jax.sharding import PartitionSpec as P

MESH = pl.DeviceIdType.MESH
BF, F32 = jnp.bfloat16, jnp.float32
TILES, CORES, K, A, VEC = 128, 2, 60, 8, 448
ALLVEC = CORES * VEC
GRP = 16
LANES = 512
HALF = TILES // CORES


def barrel(blocks):
    u = lax.broadcasted_iota(jnp.int32, blocks[0].shape, 1) // A
    for bit in (1, 2, 4, 8):
        take = (u & bit) != 0
        blocks = [jnp.where(take, blocks[(i + bit) % GRP], blocks[i]) for i in range(GRP)]
    return blocks


def kernel(t_ref, l_ref, recv2, send1, recv1, lp, lrot, part, rs1, rb1, acc2, rs2, rb2, acc3, rs3, rb3, inter, send2,
           ssem1, rsem1, lsem, rsems, agsems, ssem2, rsem2):
    me, core = lax.axis_index("tile"), lax.axis_index("chol")
    y, x, z = me // 32, lax.rem(me // 8, 4), lax.rem(me, 8)
    c_a, c_b = jnp.where(core == 0, x, y), jnp.where(core == 0, y, x)
    spin = lax.rem(me, GRP)
    own_core = lax.rem(me, CORES)
    slot = me // CORES

    def tile_at(a, b, zz):
        return jnp.where(core == 0, b * 32 + a * 8, a * 32 + b * 8) + zz

    def remote(src, dst, send_sem, recv_sem, tile, to_core=core):
        return pltpu.make_async_remote_copy(src_ref=src, dst_ref=dst, send_sem=send_sem, recv_sem=recv_sem,
                                            device_id=(tile, to_core), device_id_type=MESH)

    def shuffle(j):
        def lane_tile(m, _):
            lanes = pl.ds(pl.multiple_of(m * 128, 128), 128)
            for q in range(4):
                blocks = []
                for i in range(GRP):
                    if q * GRP + i < K:
                        block = t_ref[q * GRP + i, j, :, lanes].astype(F32)
                        blocks.append(pltpu.roll(block, A * i, 1) if i else block)
                    else:
                        blocks.append(jnp.zeros((A, 128), F32))
                blocks = barrel(blocks)
                for g in range(GRP):
                    send1[j, m * GRP + g, :, q * 128:(q + 1) * 128] = blocks[-g % GRP].astype(BF)
            return 0
        lax.fori_loop(0, TILES // GRP, lane_tile, 0)

    def start1(j, lo, hi):
        def one(q, _):
            tile = lax.rem(y + q // 32, 4) * 32 + lax.rem(x + lax.rem(q // 8, 4), 4) * 8 + lax.rem(z + lax.rem(q, 8), 8)
            src, dst = send1.at[j, tile], recv1.at[j, core, slot]
            stays = jnp.logical_and(tile == me, own_core == core)

            @pl.when(stays)
            def _():
                pltpu.make_async_copy(src, dst, rsem1.at[j]).start()

            @pl.when(jnp.logical_not(stays))
            def _():
                remote(src, dst, ssem1.at[j], rsem1.at[j], tile, own_core).start()
            return 0
        lax.fori_loop(lo, hi, one, 0)

    def start2(j, lo, hi):
        def one(q, _):
            tile = (lax.rem(y + q // 16, 4) * 32 + lax.rem(x + lax.rem(q // 4, 4), 4) * 8
                    + 2 * lax.rem(z // 2 + lax.rem(q, 4), 4) + core)
            for to_core in range(CORES):
                src, dst = send2.at[j, to_core, tile // 2], recv2.at[j, me]
                stays = jnp.logical_and(tile == me, to_core == core)

                @pl.when(stays)
                def _():
                    pltpu.make_async_copy(src, dst, rsem2.at[j]).start()

                @pl.when(jnp.logical_not(stays))
                def _():
                    remote(src, dst, ssem2.at[j], rsem2.at[j], tile, to_core).start()
            return 0
        lax.fori_loop(lo, hi, one, 0)

    def wait_bytes(ref, sem):
        pltpu.make_async_copy(ref, ref, sem).wait()

    def vectors():
        row = lax.broadcasted_iota(jnp.int32, (VEC, LANES), 0)
        column = lax.broadcasted_iota(jnp.int32, (VEC, LANES), 1)
        move = (column == row + (LANES - VEC) * core).astype(BF)
        for n in range(0, 120, 40):
            wide = jnp.dot(l_ref[n:n + 40].reshape(40 * A, VEC), move, preferred_element_type=F32)
            lp[core, n:n + 40] = wide.astype(BF).reshape(40, A, LANES)
        to_sibling = remote(lp.at[core], lp.at[core], lsem.at[0], lsem.at[1], me, 1 - core)
        to_sibling.start()
        return to_sibling

    def turn_vectors():
        def one(n, _):
            half, u = n // 64, lax.rem(n, 64)
            k = (u // GRP) * GRP + lax.rem(lax.rem(u, GRP) + GRP - spin, GRP)
            row = half * K + jnp.minimum(k, K - 1)
            left, right = lp[0, row].astype(F32), lp[1, row].astype(F32)
            whole = jnp.concatenate([left[:, :384], left[:, 384:] + right[:, :128], right[:, 128:]], axis=1)
            lrot[half, u] = jnp.where(k < K, whole, 0.0).astype(BF)
            return 0
        lax.fori_loop(0, 128, one, 0)

    def multiply1(j):
        for lo, hi in ((0, 256), (256, 512), (512, 768), (768, 896)):
            total = None
            for half in range(CORES):
                term = jnp.dot(recv1[j, half].reshape(HALF * A, LANES), lrot[half, :, :, lo:hi].reshape(LANES, hi - lo),
                               preferred_element_type=F32)
                total = term if total is None else total + term
            total = total.reshape(HALF, A, hi - lo)
            part[:, :, lo:hi] = total
            rs1[j, :, :, lo:hi] = total.astype(BF)

    def add_up(j, fill):
        copies = []

        def go(copy):
            copy.start()
            copies.append(copy)

        def arrive(first):
            for copy in copies[first:]:
                copy.wait_recv()

        for d in range(1, 4):
            a = lax.rem(c_a + d, 4)
            go(remote(rs1.at[j, pl.ds(a * 16, 16)], rb1.at[j, d - 1], rsems.at[j, 0, d - 1], rsems.at[j, 1, d - 1],
                      tile_at(a, c_b, z)))
        fill()
        arrive(0)

        def first(n, _):
            total = part[c_a * 16 + n]
            for d in range(3):
                total = total + rb1[j, d, n].astype(F32)
            acc2[n] = total
            rs2[j, n] = total.astype(BF)
            return 0
        lax.fori_loop(0, 16, first, 0)
        for d in range(1, 4):
            b = lax.rem(c_b + d, 4)
            go(remote(rs2.at[j, pl.ds(b * 4, 4)], rb2.at[j, d - 1], rsems.at[j, 0, 2 + d], rsems.at[j, 1, 2 + d],
                      tile_at(c_a, b, z)))
        fill()
        arrive(3)

        def second(n, _):
            total = acc2[c_b * 4 + n]
            for d in range(3):
                total = total + rb2[j, d, n].astype(F32)
            acc3[n] = total
            rs3[j, n] = total.astype(BF)
            return 0
        lax.fori_loop(0, 4, second, 0)
        for d in range(1, 8):
            zz = lax.rem(z + d, 8)
            go(remote(rs3.at[j, lax.rem(zz, 4)], rb3.at[j, d - 1], rsems.at[j, 0, 5 + d], rsems.at[j, 1, 5 + d],
                      tile_at(c_a, c_b, zz)))
        fill()
        arrive(6)
        total = acc3[lax.rem(z, 4)]
        for d in range(7):
            total = total + rb3[j, d].astype(F32)
        mine = c_a * 16 + c_b * 4 + lax.rem(z, 4)
        inter[j, mine] = total.astype(BF)

        def share(first, count, n, tile, source):
            src = inter.at[j, pl.ds(first, count)]
            go(remote(src, src, agsems.at[j, 0, n], agsems.at[j, 1, n], tile))
            landed.append(remote(src, inter.at[j, pl.ds(source, count)], agsems.at[j, 0, n], agsems.at[j, 1, n], tile))

        landed = []
        base = c_a * 16 + c_b * 4
        for n, d in enumerate((1, 7, 2)):
            share(mine, 1, n, tile_at(c_a, c_b, lax.rem(z + d, 8)), base + lax.rem(z + 8 - d, 4))
        fill()
        for copy in landed:
            copy.wait_recv()
        landed.clear()
        for d in range(1, 4):
            share(base, 4, 2 + d, tile_at(c_a, lax.rem(c_b + d, 4), z), c_a * 16 + lax.rem(c_b + 4 - d, 4) * 4)
        fill()
        for copy in landed:
            copy.wait_recv()
        landed.clear()
        for d in range(1, 4):
            share(c_a * 16, 16, 5 + d, tile_at(lax.rem(c_a + d, 4), c_b, z), lax.rem(c_a + 4 - d, 4) * 16)
        fill()
        for copy in landed:
            copy.wait_recv()
        return copies

    def multiply2(j):
        for half in range(CORES):
            for lo in (0, 256):
                block = lax.dot_general(inter[j].reshape(HALF * A, ALLVEC),
                                        lrot[half, lo // A:(lo + 256) // A].reshape(256, ALLVEC),
                                        (((1,), (1,)), ((), ())), preferred_element_type=F32)
                send2[j, half, :, :, lo:lo + 256] = block.astype(BF).reshape(HALF, A, 256)

    class Filler:
        def __init__(self, begin, cuts):
            self.begin, self.cuts = begin, cuts

        def __call__(self):
            lo = self.cuts.pop(0)
            self.begin(lo, self.cuts[0])

    shuffle(0)
    start1(0, 0, TILES)
    to_sibling = vectors()
    shuffle(1)
    to_sibling.wait_recv()
    turn_vectors()
    fill1 = Filler(lambda lo, hi: start1(1, lo, hi), [0, 32, 52, 68, 84, 100, 116, 128])
    fill1()
    wait_bytes(recv1.at[0], rsem1.at[0])
    multiply1(0)
    copies = add_up(0, fill1)
    multiply2(0)
    fill2 = Filler(lambda lo, hi: start2(0, lo, hi), [0, 16, 26, 34, 42, 50, 58, 64])
    fill2()
    wait_bytes(recv1.at[1], rsem1.at[1])
    multiply1(1)
    copies += add_up(1, fill2)
    multiply2(1)
    start2(1, 0, HALF)
    for j in range(2):
        wait_bytes(recv2.at[j], rsem2.at[j])
    for copy in copies + [to_sibling]:
        copy.wait_send()
    for j in range(2):
        @pl.when(own_core == core)
        def _():
            wait_bytes(send1.at[j, pl.ds(0, TILES - 1)], ssem1.at[j])
            wait_bytes(recv2.at[j, pl.ds(0, TILES - 1)], ssem2.at[j])

        @pl.when(own_core != core)
        def _():
            wait_bytes(send1.at[j], ssem1.at[j])
            wait_bytes(recv2.at[j], ssem2.at[j])


def unshuffle(r_ref, o_ref):
    for j in range(2):
        for q in range(4):
            blocks = [r_ref[j, g, :, q * 128:(q + 1) * 128].astype(F32) for g in range(GRP)]
            blocks = barrel(blocks)
            for i in range(min(GRP, K - q * GRP)):
                block = blocks[-i % GRP]
                o_ref[q * GRP + i, j] = (pltpu.roll(block, 128 - A * i, 1) if i else block).astype(BF)


def shards(amplitudes, cholesky):
    vmem = pl.BlockSpec(memory_space=pltpu.VMEM)
    dma, V = pltpu.SemaphoreType.DMA, pltpu.VMEM
    landed = pl.pallas_call(
        kernel,
        out_shape=jax.ShapeDtypeStruct((2, TILES, A, LANES), BF),
        in_specs=[vmem, vmem],
        out_specs=pl.BlockSpec(memory_space=pl.ANY),
        scratch_shapes=[
            V((2, TILES, A, LANES), BF), V((2, CORES, HALF, A, LANES), BF), V((CORES, 120, A, LANES), BF),
            V((CORES, 64, A, ALLVEC), BF), V((HALF, A, ALLVEC), F32), V((2, HALF, A, ALLVEC), BF),
            V((2, 3, 16, A, ALLVEC), BF), V((16, A, ALLVEC), F32), V((2, 16, A, ALLVEC), BF),
            V((2, 3, 4, A, ALLVEC), BF), V((4, A, ALLVEC), F32), V((2, 4, A, ALLVEC), BF),
            V((2, 7, A, ALLVEC), BF), V((2, HALF, A, ALLVEC), BF), V((2, CORES, HALF, A, LANES), BF),
            dma((2,)), dma((2,)), dma((2,)), dma((2, 2, 13)), dma((2, 2, 9)), dma((2,)), dma((2,)),
        ],
        compiler_params=pltpu.CompilerParams(has_side_effects=True, vmem_limit_bytes=56 * 2**20),
    )(amplitudes, cholesky)
    return pl.pallas_call(
        unshuffle,
        grid=(TILES // GRP,),
        out_shape=jax.ShapeDtypeStruct(amplitudes.shape, BF),
        in_specs=[pl.BlockSpec((2, GRP, A, LANES), lambda m: (0, m, 0, 0))],
        out_specs=pl.BlockSpec((K, 2, A, 128), lambda m: (0, 0, 0, m)),
    )(landed)


def solution(mesh):
    in_specs = (P("chol", None, "tile", None), P(None, "tile", "chol"))
    out_specs = P("chol", None, "tile", None)
    return jax.shard_map(shards, mesh=mesh, in_specs=in_specs, out_specs=out_specs, check_vma=False)
```

time: 505 us -> 179 us (0.35)
  blocking collectives: 199 us -> 0 us
  Pallas kernels: 0 us -> 176 us
  waiting for transfers between devices: 152 us -> 0 us
  local copies, waits for them, and re-layouts: 114 us -> 2.59 us
  starting transfers between devices: 16.6 us -> 0 us
  between operations: 13.5 us -> 0.01 us
  matrix products: 9.4 us -> 0 us
    pallas_call x0 -> x2, Pallas kernels: none -> 176 us  [the longest x1 170 us: shards(): pl.pallas_call(kernel, out_shape=jax.ShapeDtypeStruct((2, TILES, A, LANES...]
    unnamed x1 -> x0, blocking collectives: 138 us -> none
    all_gather x2 -> x0, waiting for transfers between devices: 130 us -> none  [the longest x1 111 us: shards(): lax.all_gather(shared_rows, ('tile', 'chol'), axis=0, tiled=True)]
    unnamed x9 -> x1, local copies, waits for them, and re-layouts: 72 us -> 2.59 us
    all_to_all x1 -> x0, blocking collectives: 60.2 us -> none  [shards(): lax.all_to_all(local_cycle, 'tile', split_axis=2, concat_axis=3, tiled=True)]
    all_to_all x4 -> x0, local copies, waits for them, and re-layouts: 22.9 us -> none  [the longest x2 11.8 us: shards(): lax.all_to_all(amplitudes, 'tile', split_axis=3, concat_axis=2, tiled=True)]
    all_to_all x1 -> x0, waiting for transfers between devices: 22.7 us -> none  [shards(): lax.all_to_all(amplitudes, 'tile', split_axis=3, concat_axis=2, tiled=True)]
    all_to_all x1 -> x0, starting transfers between devices: 16.3 us -> none  [shards(): lax.all_to_all(amplitudes, 'tile', split_axis=3, concat_axis=2, tiled=True)]
  transfers between devices with their start and end apart: 3 -> 0, of which waited for: 3 -> 0; matrix products, arithmetic and copies ran while one was open for 2% -> 0% of each run, Pallas kernels for 0% -> 0%
where the time goes in v1:
time: 179 us
  Pallas kernels  176 us (98%)
  local copies, waits for them, and re-layouts  2.59 us (1%)
    pallas_call x1, Pallas kernels, shards(): pl.pallas_call(kernel, out_shape=jax.ShapeDtypeStruct((2, TILES, A, LANES...  170 us
    pallas_call x1, Pallas kernels, shards(): pl.pallas_call(unshuffle, grid=(TILES // GRP,), out_shape=jax.ShapeDtypeS...  6.16 us

profile of v1, /device:TPU:1, one launch (start us, length us, event | category | flops | bytes accessed | tf_op | source)
XLA Modules:
  0.0 179.0 jit_solution(10394030045538308149)
XLA Ops:
  0.0 2.6 %copy.3.l_ref = bf16[120,8,448]{2,1,0:T(8,128)(2,1)} copy(bf16[120,8,448]{0,2,1:T(8,128)(2,1)} %param.3) | data formatting | bytes 1720320 | tf_op args[1]
  2.6 170.3 %shard_map.28.r_ref = bf16[2,128,8,512]{3,2,1,0:T(8,128)(2,1)} custom-call(bf16[60,2,8,1024]{3,2,1,0:T(8,128)(2,1)} %t_ref.1, bf16[120,8,448]{2,1,0:T(8,128)(2,1)} %copy.3.l_ref), custom_call_target="tpu_custom_call" | custom-call | tf_op jit(solution)/shard_map/pallas_call | solution.py:273
  172.9 6.2 %shard_map.29 = bf16[60,2,8,1024]{3,2,1,0:T(8,128)(2,1)} custom-call(bf16[2,128,8,512]{3,2,1,0:T(8,128)(2,1)} %shard_map.28.r_ref), custom_call_target="tpu_custom_call" | custom-call | tf_op jit(solution)/shard_map/pallas_call | solution.py:288

commit v2 on v0

v2 whole, which is shorter than its diff:
```python
import jax
import jax.numpy as jnp
from jax import lax
from jax.experimental import pallas as pl
from jax.experimental.pallas import tpu as pltpu
from jax.sharding import PartitionSpec as P

MESH = pl.DeviceIdType.MESH
BF, F32 = jnp.bfloat16, jnp.float32
K, VEC = 60, 448
COLS, DEPTH = 16, 8
CUTS, CUT = 5, 12
WIDE = CUT * 64
SUBS, SUB = 4, 15
MAIN, EDGE = 384, 128


def kernel(t_ref, l_ref, out_ref, slab_a, slab_b, slab_c, edge, edge_in, send1, recv1, part, rs_a, rs_bc, rb_a, rb_bc,
           inter_a, inter_bc, send2, recv2, staged, own_sem, swap_send, edge_sem, ring_send, ring_recv, t_send, t_recv,
           sum_send, sum_recv, share_send, share_recv, r_send, r_recv, out_sem):
    me, core = lax.axis_index("tile"), lax.axis_index("chol")
    w, z = me // DEPTH, lax.rem(me, DEPTH)
    y, x = w // 4, lax.rem(w, 4)
    slabs = (slab_a, slab_b, slab_c)

    def plane(q):
        return lax.rem(y + q // 4, 4) * 4 + lax.rem(x + lax.rem(q, 4), 4)

    def level(d):
        return lax.rem(z + d + DEPTH, DEPTH)

    def remote(src, dst, send_sem, recv_sem, tile, to_core):
        return pltpu.make_async_remote_copy(src_ref=src, dst_ref=dst, send_sem=send_sem, recv_sem=recv_sem,
                                            device_id=(tile, to_core), device_id_type=MESH)

    def wait_bytes(ref, sem):
        pltpu.make_async_copy(ref, ref, sem).wait()

    barrier = pltpu.get_barrier_semaphore()

    def greet(q, _):
        pl.semaphore_signal(barrier, inc=1, device_id=(plane(q // 2) * DEPTH + z, lax.rem(core + q, 2)),
                            device_id_type=MESH)
        return 0
    lax.fori_loop(1, 2 * COLS, greet, 0)
    for d in (-1, 1):
        pl.semaphore_signal(barrier, inc=1, device_id=(w * DEPTH + level(d), core), device_id_type=MESH)

    def vectors(own, where, sem):
        def begin():
            for half in range(2):
                src = l_ref.at[pl.ds(half * K, K), :, pl.ds(0, MAIN)]
                if half == own:
                    pltpu.make_async_copy(src, where.at[:, z], sem).start()
                else:
                    remote(src, where.at[:, z], swap_send.at[0], sem, me, 1 - core).start()
        pl.when(core == own)(begin)

    row = lax.broadcasted_iota(jnp.int32, (VEC - MAIN, EDGE), 0)
    column = lax.broadcasted_iota(jnp.int32, (VEC - MAIN, EDGE), 1)
    place = (column == row + (VEC - MAIN) * core).astype(BF)
    tail = jnp.dot(l_ref[:, :, MAIN:].reshape(2 * K * 8, VEC - MAIN), place, preferred_element_type=F32)
    edge[...] = tail.astype(BF).reshape(2 * K, 8, EDGE)

    pl.semaphore_wait(barrier, 2 * COLS + 1)

    vectors(0, slab_a, own_sem.at[0])
    vectors(1, slab_b, own_sem.at[1])
    to_sibling = remote(edge.at[pl.ds((1 - core) * K, K)], edge_in, edge_sem.at[0], edge_sem.at[1], me, 1 - core)
    to_sibling.start()

    sent = []

    def ring(p, hop):
        slab = slabs[p]
        for sub in range(SUBS):
            for way in range(2):
                if hop == 3 and sub % 2 != way:
                    continue
                if hop:
                    arrived(p, sub, way, hop - 1)
                step = -hop if way == 0 else hop
                block = slab.at[pl.ds(sub * SUB, SUB), level(step)]
                n = ((p * SUBS + sub) * 2 + way) * 4 + hop
                copy = remote(block, block, ring_send.at[n], ring_recv.at[n],
                              w * DEPTH + level(1 if way == 0 else -1), core)
                copy.start()
                sent.append(copy)

    def arrived(p, sub, way, hop):
        step = -1 - hop if way == 0 else 1 + hop
        n = ((p * SUBS + sub) * 2 + way) * 4 + hop
        wait_bytes(slabs[p].at[pl.ds(sub * SUB, SUB), level(step)], ring_recv.at[n])

    def last(p):
        for sub in range(SUBS):
            arrived(p, sub, 1 - sub % 2, 2)
            arrived(p, sub, sub % 2, 3)

    low = lax.broadcasted_iota(jnp.int32, (16, 128), 1) < 64

    def halves(first, second):
        return (jnp.where(low, first, pltpu.roll(second, 64, 1)), jnp.where(low, pltpu.roll(first, 64, 1), second))

    def shuffle(n):
        def lane_tile(m, _):
            lanes = pl.ds(pl.multiple_of(m * 128, 128), 128)
            for pair in range(CUT // 2):
                k = n * CUT + 2 * pair
                for side, block in enumerate(halves(t_ref[k, :, lanes].astype(F32), t_ref[k + 1, :, lanes].astype(F32))):
                    send1[n, 2 * m + side, :, pair * 128:(pair + 1) * 128] = block.astype(BF)
            return 0
        lax.fori_loop(0, COLS // 2, lane_tile, 0)

    def unshuffle(n):
        def lane_tile(m, _):
            lanes = pl.ds(pl.multiple_of(m * 128, 128), 128)
            for pair in range(CUT // 2):
                here = slice(pair * 128, (pair + 1) * 128)
                k = n * CUT + 2 * pair
                for side, block in enumerate(halves(recv2[n, 2 * m, :, here].astype(F32),
                                                    recv2[n, 2 * m + 1, :, here].astype(F32))):
                    staged[k + side, :, lanes] = block.astype(BF)
            return 0
        lax.fori_loop(0, COLS // 2, lane_tile, 0)

    def exchange(n, send, recv, send_sem, recv_sem):
        pltpu.make_async_copy(send.at[n, w], recv.at[n, w], recv_sem.at[n]).start()

        def one(q, _):
            to = plane(q)
            remote(send.at[n, to], recv.at[n, w], send_sem.at[n], recv_sem.at[n], to * DEPTH + z, core).start()
            return 0
        lax.fori_loop(1, COLS, one, 0)

    def multiply1(slab, width, rs, lo):
        total = None
        for n in range(CUTS):
            term = jnp.dot(recv1[n].reshape(256, WIDE), slab[n * CUT:(n + 1) * CUT].reshape(WIDE, width),
                           preferred_element_type=F32)
            total = term if total is None else total + term
        total = total.reshape(COLS, 2, 8, width)
        part[:, :, :, lo:lo + width] = total
        rs[:, :, :, lo:lo + width] = total.astype(BF)

    def add_up(i, rs, rb):
        def one(q, _):
            to, to_core = plane(q // 2), lax.rem(core + q, 2)
            remote(rs.at[to, to_core], rb.at[q - 1], sum_send.at[i], sum_recv.at[i], to * DEPTH + z, to_core).start()
            return 0
        lax.fori_loop(1, 2 * COLS, one, 0)

    def share(i, rb, inter, width):
        wait_bytes(rb, sum_recv.at[i])
        total = part[w, core, :, :width]
        for n in range(2 * COLS - 1):
            total = total + rb[n].astype(F32)
        inter[w, core] = total.astype(BF)

        def one(q, _):
            to, to_core = plane(q // 2), lax.rem(core + q, 2)
            block = inter.at[w, core]
            remote(block, block, share_send.at[i], share_recv.at[i], to * DEPTH + z, to_core).start()
            return 0
        lax.fori_loop(1, 2 * COLS, one, 0)

    def multiply2(n):
        def times(rows, slab, width):
            return lax.dot_general(rows.reshape(256, width), slab[n * CUT:(n + 1) * CUT].reshape(WIDE, width),
                                   (((1,), (1,)), ((), ())), preferred_element_type=F32)
        total = times(inter_a[...], slab_a, MAIN)
        total = total + times(inter_bc[:, :, :, :MAIN], slab_b, MAIN)
        total = total + times(inter_bc[:, :, :, MAIN:], slab_c, EDGE)
        send2[n] = total.astype(BF).reshape(COLS, 16, WIDE)

    wait_bytes(slab_a.at[:, z], own_sem.at[0])
    ring(0, 0)
    for n in range(CUTS):
        shuffle(n)
        exchange(n, send1, recv1, t_send, t_recv)
    to_sibling.wait_recv()

    def merge(k, _):
        slab_c[k, z] = (edge[core * K + k].astype(F32) + edge_in[k].astype(F32)).astype(BF)
        return 0
    lax.fori_loop(0, K, merge, 0)
    ring(0, 1)
    ring(0, 2)
    ring(0, 3)
    wait_bytes(slab_b.at[:, z], own_sem.at[1])
    ring(1, 0)
    ring(2, 0)
    last(0)
    for n in range(CUTS):
        wait_bytes(recv1.at[n], t_recv.at[n])
    multiply1(slab_a, MAIN, rs_a, 0)
    add_up(0, rs_a, rb_a)
    ring(1, 1)
    ring(2, 1)
    share(0, rb_a, inter_a, MAIN)
    ring(1, 2)
    ring(2, 2)
    ring(1, 3)
    ring(2, 3)
    last(1)
    multiply1(slab_b, MAIN, rs_bc, 0)
    last(2)
    multiply1(slab_c, EDGE, rs_bc, MAIN)
    add_up(1, rs_bc, rb_bc)
    wait_bytes(rb_a, share_recv.at[0])
    share(1, rb_bc, inter_bc, MAIN + EDGE)
    wait_bytes(rb_bc, share_recv.at[1])
    for n in range(CUTS):
        multiply2(n)
        exchange(n, send2, recv2, r_send, r_recv)
    for n in range(CUTS):
        wait_bytes(recv2.at[n], r_recv.at[n])
        unshuffle(n)
        pltpu.make_async_copy(staged.at[pl.ds(n * CUT, CUT)], out_ref.at[pl.ds(n * CUT, CUT)], out_sem.at[n]).start()

    for copy in sent + [to_sibling]:
        copy.wait_send()
    wait_bytes(slab_a.at[:, z], swap_send.at[0])
    for n in range(CUTS):
        wait_bytes(recv1.at[n, pl.ds(0, COLS - 1)], t_send.at[n])
        wait_bytes(recv2.at[n, pl.ds(0, COLS - 1)], r_send.at[n])
    for i, rb in enumerate((rb_a, rb_bc)):
        wait_bytes(rb, sum_send.at[i])
        wait_bytes(rb, share_send.at[i])
    for n in range(CUTS):
        wait_bytes(staged.at[pl.ds(n * CUT, CUT)], out_sem.at[n])


def shards(amplitudes, cholesky):
    vmem = pl.BlockSpec(memory_space=pltpu.VMEM)
    dma, V = pltpu.SemaphoreType.DMA, pltpu.VMEM
    both = MAIN + EDGE
    out = pl.pallas_call(
        kernel,
        out_shape=jax.ShapeDtypeStruct((K, 16, 1024), BF),
        in_specs=[vmem, vmem],
        out_specs=pl.BlockSpec(memory_space=pl.ANY),
        scratch_shapes=[
            V((K, DEPTH, 8, MAIN), BF), V((K, DEPTH, 8, MAIN), BF), V((K, DEPTH, 8, EDGE), BF),
            V((2 * K, 8, EDGE), BF), V((K, 8, EDGE), BF),
            V((CUTS, COLS, 16, WIDE), BF), V((CUTS, COLS, 16, WIDE), BF),
            V((COLS, 2, 8, both), F32), V((COLS, 2, 8, MAIN), BF), V((COLS, 2, 8, both), BF),
            V((2 * COLS - 1, 8, MAIN), BF), V((2 * COLS - 1, 8, both), BF),
            V((COLS, 2, 8, MAIN), BF), V((COLS, 2, 8, both), BF),
            V((CUTS, COLS, 16, WIDE), BF), V((CUTS, COLS, 16, WIDE), BF), V((K, 16, 1024), BF),
            dma((2,)), dma((1,)), dma((2,)), dma((96,)), dma((96,)), dma((CUTS,)), dma((CUTS,)),
            dma((2,)), dma((2,)), dma((2,)), dma((2,)), dma((CUTS,)), dma((CUTS,)), dma((CUTS,)),
        ],
        compiler_params=pltpu.CompilerParams(has_side_effects=True, collective_id=0, vmem_limit_bytes=56 * 2**20),
    )(amplitudes.reshape(K, 16, 1024), cholesky)
    return out.reshape(amplitudes.shape)


def solution(mesh):
    in_specs = (P("chol", None, "tile", None), P(None, "tile", "chol"))
    out_specs = P("chol", None, "tile", None)
    return jax.shard_map(shards, mesh=mesh, in_specs=in_specs, out_specs=out_specs, check_vma=False)
```

time: 505 us -> 127 us (0.25)
  blocking collectives: 199 us -> 0 us
  waiting for transfers between devices: 152 us -> 0 us
  Pallas kernels: 0 us -> 121 us
  local copies, waits for them, and re-layouts: 114 us -> 5.69 us
  starting transfers between devices: 16.6 us -> 0 us
  between operations: 13.5 us -> 0.01 us
  matrix products: 9.4 us -> 0 us
    unnamed x1 -> x0, blocking collectives: 138 us -> none
    all_gather x2 -> x0, waiting for transfers between devices: 130 us -> none  [the longest x1 111 us: shards(): lax.all_gather(shared_rows, ('tile', 'chol'), axis=0, tiled=True)]
    pallas_call x0 -> x1, Pallas kernels: none -> 121 us  [shards(): pl.pallas_call(kernel, out_shape=jax.ShapeDtypeStruct((K, 16, 1024), BF),...]
    unnamed x9 -> x2, local copies, waits for them, and re-layouts: 72 us -> 5.69 us
    all_to_all x1 -> x0, blocking collectives: 60.2 us -> none  [shards(): lax.all_to_all(local_cycle, 'tile', split_axis=2, concat_axis=3, tiled=True)]
    all_to_all x4 -> x0, local copies, waits for them, and re-layouts: 22.9 us -> none  [the longest x2 11.8 us: shards(): lax.all_to_all(amplitudes, 'tile', split_axis=3, concat_axis=2, tiled=True)]
    all_to_all x1 -> x0, waiting for transfers between devices: 22.7 us -> none  [shards(): lax.all_to_all(amplitudes, 'tile', split_axis=3, concat_axis=2, tiled=True)]
    all_to_all x1 -> x0, starting transfers between devices: 16.3 us -> none  [shards(): lax.all_to_all(amplitudes, 'tile', split_axis=3, concat_axis=2, tiled=True)]
  transfers between devices with their start and end apart: 3 -> 0, of which waited for: 3 -> 0; matrix products, arithmetic and copies ran while one was open for 2% -> 0% of each run, Pallas kernels for 0% -> 0%
where the time goes in v2:
time: 127 us
  Pallas kernels  121 us (95%)
  local copies, waits for them, and re-layouts  5.69 us (4%)
    pallas_call x1, Pallas kernels, shards(): pl.pallas_call(kernel, out_shape=jax.ShapeDtypeStruct((K, 16, 1024), BF),...  121 us
    unnamed x2, local copies, waits for them, and re-layouts  5.69 us

profile of v2, /device:TPU:1, one launch (start us, length us, event | category | flops | bytes accessed | tf_op | source)
XLA Modules:
  0.0 127.0 jit_solution(3313561580701764009)
XLA Ops:
  0.0 2.6 %copy.3.l_ref = bf16[120,8,448]{2,1,0:T(8,128)(2,1)} copy(bf16[120,8,448]{0,2,1:T(8,128)(2,1)} %param.3) | data formatting | bytes 1720320 | tf_op args[1]
  2.6 121.3 %shard_map.28 = bf16[60,16,1024]{2,1,0:T(8,128)(2,1)} custom-call(bf16[60,16,1024]{2,1,0:T(8,128)(2,1)} %bitcast.3, bf16[120,8,448]{2,1,0:T(8,128)(2,1)} %copy.3.l_ref), custom_call_target="tpu_custom_call" | custom-call | tf_op jit(solution)/shard_map/pallas_call | solution.py:238
  123.9 3.1 %copy.5 = bf16[60,2,8,1024]{3,2,1,0:T(8,128)(2,1)} copy(bf16[60,2,8,1024]{3,2,1,0:T(8,128)(2,1)} %bitcast.2) | data formatting | bytes 3932160

commit v3 on v2

--- a/solution.py
+++ b/solution.py
@@ -15,13 +15,18 @@
 MAIN, EDGE = 384, 128
 
 
-def kernel(t_ref, l_ref, out_ref, slab_a, slab_b, slab_c, edge, edge_in, send1, recv1, part, rs_a, rs_bc, rb_a, rb_bc,
-           inter_a, inter_bc, send2, recv2, staged, own_sem, swap_send, edge_sem, ring_send, ring_recv, t_send, t_recv,
-           sum_send, sum_recv, share_send, share_recv, r_send, r_recv, out_sem):
+def kernel(t_hbm, l_hbm, out_ref, t_ref, l_ref, slab_a, slab_b, slab_c, edge, edge_in, send1, recv1, part_a, part_b, part_c,
+           rs_a, rs_b, rs_c, rb_a, rb_b, rb_c, inter_a, inter_b, inter_c, send2, recv2, own_sem, swap_send, edge_sem,
+           ring_send, ring_recv, t_send, t_recv, sum_send, sum_recv, share_send, share_recv, r_send, r_recv, in_sem):
+    load_l = pltpu.make_async_copy(l_hbm, l_ref, in_sem.at[0])
+    load_l.start()
+    load_t = pltpu.make_async_copy(t_hbm, t_ref, in_sem.at[1])
+    load_t.start()
     me, core = lax.axis_index("tile"), lax.axis_index("chol")
     w, z = me // DEPTH, lax.rem(me, DEPTH)
     y, x = w // 4, lax.rem(w, 4)
-    slabs = (slab_a, slab_b, slab_c)
+    slabs, widths = (slab_a, slab_b, slab_c), (MAIN, MAIN, EDGE)
+    parts, rss, rbs, inters = (part_a, part_b, part_c), (rs_a, rs_b, rs_c), (rb_a, rb_b, rb_c), (inter_a, inter_b, inter_c)
 
     def plane(q):
         return lax.rem(y + q // 4, 4) * 4 + lax.rem(x + lax.rem(q, 4), 4)
@@ -49,26 +54,17 @@
     def vectors(own, where, sem):
         def begin():
             for half in range(2):
-                src = l_ref.at[pl.ds(half * K, K), :, pl.ds(0, MAIN)]
+                src = l_hbm.at[pl.ds(half * K, K), :, pl.ds(0, MAIN)]
                 if half == own:
                     pltpu.make_async_copy(src, where.at[:, z], sem).start()
                 else:
                     remote(src, where.at[:, z], swap_send.at[0], sem, me, 1 - core).start()
         pl.when(core == own)(begin)
 
-    row = lax.broadcasted_iota(jnp.int32, (VEC - MAIN, EDGE), 0)
-    column = lax.broadcasted_iota(jnp.int32, (VEC - MAIN, EDGE), 1)
-    place = (column == row + (VEC - MAIN) * core).astype(BF)
-    tail = jnp.dot(l_ref[:, :, MAIN:].reshape(2 * K * 8, VEC - MAIN), place, preferred_element_type=F32)
-    edge[...] = tail.astype(BF).reshape(2 * K, 8, EDGE)
-
     pl.semaphore_wait(barrier, 2 * COLS + 1)
 
     vectors(0, slab_a, own_sem.at[0])
     vectors(1, slab_b, own_sem.at[1])
-    to_sibling = remote(edge.at[pl.ds((1 - core) * K, K)], edge_in, edge_sem.at[0], edge_sem.at[1], me, 1 - core)
-    to_sibling.start()
-
     sent = []
 
     def ring(p, hop):
@@ -120,7 +116,7 @@
                 k = n * CUT + 2 * pair
                 for side, block in enumerate(halves(recv2[n, 2 * m, :, here].astype(F32),
                                                     recv2[n, 2 * m + 1, :, here].astype(F32))):
-                    staged[k + side, :, lanes] = block.astype(BF)
+                    out_ref[k + side, :, lanes] = block.astype(BF)
             return 0
         lax.fori_loop(0, COLS // 2, lane_tile, 0)
 
@@ -133,48 +129,59 @@
             return 0
         lax.fori_loop(1, COLS, one, 0)
 
-    def multiply1(slab, width, rs, lo):
+    def multiply1(p):
+        slab, width = slabs[p], widths[p]
         total = None
         for n in range(CUTS):
             term = jnp.dot(recv1[n].reshape(256, WIDE), slab[n * CUT:(n + 1) * CUT].reshape(WIDE, width),
                            preferred_element_type=F32)
             total = term if total is None else total + term
         total = total.reshape(COLS, 2, 8, width)
-        part[:, :, :, lo:lo + width] = total
-        rs[:, :, :, lo:lo + width] = total.astype(BF)
-
-    def add_up(i, rs, rb):
+        parts[p][...] = total
+        rss[p][...] = total.astype(BF)
+
+    def add_up(p):
         def one(q, _):
             to, to_core = plane(q // 2), lax.rem(core + q, 2)
-            remote(rs.at[to, to_core], rb.at[q - 1], sum_send.at[i], sum_recv.at[i], to * DEPTH + z, to_core).start()
+            remote(rss[p].at[to, to_core], rbs[p].at[q - 1], sum_send.at[p], sum_recv.at[p], to * DEPTH + z,
+                   to_core).start()
             return 0
         lax.fori_loop(1, 2 * COLS, one, 0)
 
-    def share(i, rb, inter, width):
-        wait_bytes(rb, sum_recv.at[i])
-        total = part[w, core, :, :width]
+    def share(p):
+        wait_bytes(rbs[p], sum_recv.at[p])
+        total = parts[p][w, core]
         for n in range(2 * COLS - 1):
-            total = total + rb[n].astype(F32)
-        inter[w, core] = total.astype(BF)
+            total = total + rbs[p][n].astype(F32)
+        inters[p][w, core] = total.astype(BF)
 
         def one(q, _):
             to, to_core = plane(q // 2), lax.rem(core + q, 2)
-            block = inter.at[w, core]
-            remote(block, block, share_send.at[i], share_recv.at[i], to * DEPTH + z, to_core).start()
+            block = inters[p].at[w, core]
+            remote(block, block, share_send.at[p], share_recv.at[p], to * DEPTH + z, to_core).start()
             return 0
         lax.fori_loop(1, 2 * COLS, one, 0)
 
     def multiply2(n):
-        def times(rows, slab, width):
-            return lax.dot_general(rows.reshape(256, width), slab[n * CUT:(n + 1) * CUT].reshape(WIDE, width),
-                                   (((1,), (1,)), ((), ())), preferred_element_type=F32)
-        total = times(inter_a[...], slab_a, MAIN)
-        total = total + times(inter_bc[:, :, :, :MAIN], slab_b, MAIN)
-        total = total + times(inter_bc[:, :, :, MAIN:], slab_c, EDGE)
+        total = None
+        for p in range(3):
+            rows = slabs[p][n * CUT:(n + 1) * CUT].reshape(WIDE, widths[p])
+            term = lax.dot_general(inters[p][...].reshape(256, widths[p]), rows, (((1,), (1,)), ((), ())),
+                                   preferred_element_type=F32)
+            total = term if total is None else total + term
         send2[n] = total.astype(BF).reshape(COLS, 16, WIDE)
 
     wait_bytes(slab_a.at[:, z], own_sem.at[0])
     ring(0, 0)
+    load_l.wait()
+    row = lax.broadcasted_iota(jnp.int32, (VEC - MAIN, EDGE), 0)
+    column = lax.broadcasted_iota(jnp.int32, (VEC - MAIN, EDGE), 1)
+    place = (column == row + (VEC - MAIN) * core).astype(BF)
+    tail = jnp.dot(l_ref[:, :, MAIN:].reshape(2 * K * 8, VEC - MAIN), place, preferred_element_type=F32)
+    edge[...] = tail.astype(BF).reshape(2 * K, 8, EDGE)
+    to_sibling = remote(edge.at[pl.ds((1 - core) * K, K)], edge_in, edge_sem.at[0], edge_sem.at[1], me, 1 - core)
+    to_sibling.start()
+    load_t.wait()
     for n in range(CUTS):
         shuffle(n)
         exchange(n, send1, recv1, t_send, t_recv)
@@ -193,30 +200,31 @@
     last(0)
     for n in range(CUTS):
         wait_bytes(recv1.at[n], t_recv.at[n])
-    multiply1(slab_a, MAIN, rs_a, 0)
-    add_up(0, rs_a, rb_a)
+    multiply1(0)
+    add_up(0)
     ring(1, 1)
     ring(2, 1)
-    share(0, rb_a, inter_a, MAIN)
+    share(0)
     ring(1, 2)
     ring(2, 2)
     ring(1, 3)
     ring(2, 3)
     last(1)
-    multiply1(slab_b, MAIN, rs_bc, 0)
+    multiply1(1)
+    add_up(1)
     last(2)
-    multiply1(slab_c, EDGE, rs_bc, MAIN)
-    add_up(1, rs_bc, rb_bc)
-    wait_bytes(rb_a, share_recv.at[0])
-    share(1, rb_bc, inter_bc, MAIN + EDGE)
-    wait_bytes(rb_bc, share_recv.at[1])
+    multiply1(2)
+    add_up(2)
+    share(1)
+    share(2)
+    for p in range(3):
+        wait_bytes(rbs[p], share_recv.at[p])
     for n in range(CUTS):
         multiply2(n)
         exchange(n, send2, recv2, r_send, r_recv)
     for n in range(CUTS):
         wait_bytes(recv2.at[n], r_recv.at[n])
         unshuffle(n)
-        pltpu.make_async_copy(staged.at[pl.ds(n * CUT, CUT)], out_ref.at[pl.ds(n * CUT, CUT)], out_sem.at[n]).start()
 
     for copy in sent + [to_sibling]:
         copy.wait_send()
@@ -224,34 +232,31 @@
     for n in range(CUTS):
         wait_bytes(recv1.at[n, pl.ds(0, COLS - 1)], t_send.at[n])
         wait_bytes(recv2.at[n, pl.ds(0, COLS - 1)], r_send.at[n])
-    for i, rb in enumerate((rb_a, rb_bc)):
-        wait_bytes(rb, sum_send.at[i])
-        wait_bytes(rb, share_send.at[i])
-    for n in range(CUTS):
-        wait_bytes(staged.at[pl.ds(n * CUT, CUT)], out_sem.at[n])
+    for p in range(3):
+        wait_bytes(rbs[p], sum_send.at[p])
+        wait_bytes(rbs[p], share_send.at[p])
 
 
 def shards(amplitudes, cholesky):
-    vmem = pl.BlockSpec(memory_space=pltpu.VMEM)
     dma, V = pltpu.SemaphoreType.DMA, pltpu.VMEM
-    both = MAIN + EDGE
+    widths = (MAIN, MAIN, EDGE)
     out = pl.pallas_call(
         kernel,
         out_shape=jax.ShapeDtypeStruct((K, 16, 1024), BF),
-        in_specs=[vmem, vmem],
-        out_specs=pl.BlockSpec(memory_space=pl.ANY),
+        in_specs=[pl.BlockSpec(memory_space=pl.ANY)] * 2,
+        out_specs=pl.BlockSpec(memory_space=pltpu.VMEM),
         scratch_shapes=[
-            V((K, DEPTH, 8, MAIN), BF), V((K, DEPTH, 8, MAIN), BF), V((K, DEPTH, 8, EDGE), BF),
+            V((K, 16, 1024), BF), V((2 * K, 8, VEC), BF),
+            *[V((K, DEPTH, 8, n), BF) for n in widths],
             V((2 * K, 8, EDGE), BF), V((K, 8, EDGE), BF),
             V((CUTS, COLS, 16, WIDE), BF), V((CUTS, COLS, 16, WIDE), BF),
-            V((COLS, 2, 8, both), F32), V((COLS, 2, 8, MAIN), BF), V((COLS, 2, 8, both), BF),
-            V((2 * COLS - 1, 8, MAIN), BF), V((2 * COLS - 1, 8, both), BF),
-            V((COLS, 2, 8, MAIN), BF), V((COLS, 2, 8, both), BF),
-            V((CUTS, COLS, 16, WIDE), BF), V((CUTS, COLS, 16, WIDE), BF), V((K, 16, 1024), BF),
+            *[V((COLS, 2, 8, n), F32) for n in widths], *[V((COLS, 2, 8, n), BF) for n in widths],
+            *[V((2 * COLS - 1, 8, n), BF) for n in widths], *[V((COLS, 2, 8, n), BF) for n in widths],
+            V((CUTS, COLS, 16, WIDE), BF), V((CUTS, COLS, 16, WIDE), BF),
             dma((2,)), dma((1,)), dma((2,)), dma((96,)), dma((96,)), dma((CUTS,)), dma((CUTS,)),
-            dma((2,)), dma((2,)), dma((2,)), dma((2,)), dma((CUTS,)), dma((CUTS,)), dma((CUTS,)),
+            dma((3,)), dma((3,)), dma((3,)), dma((3,)), dma((CUTS,)), dma((CUTS,)), dma((2,)),
         ],
-        compiler_params=pltpu.CompilerParams(has_side_effects=True, collective_id=0, vmem_limit_bytes=56 * 2**20),
+        compiler_params=pltpu.CompilerParams(has_side_effects=True, collective_id=0, vmem_limit_bytes=44 * 2**20),
     )(amplitudes.reshape(K, 16, 1024), cholesky)
     return out.reshape(amplitudes.shape)
 

time: 127 us -> 124 us (0.976)
    pallas_call x1, Pallas kernels: 121 us -> 120 us  [shards(): pl.pallas_call(kernel, out_shape=jax.ShapeDtypeStruct((K, 16, 1024), BF),...]
    unnamed x2 -> x4, local copies, waits for them, and re-layouts: 5.69 us -> 4.65 us
where the time goes in v3:
time: 124 us
  Pallas kernels  120 us (97%)
  local copies, waits for them, and re-layouts  4.65 us (4%)
    pallas_call x1, Pallas kernels, shards(): pl.pallas_call(kernel, out_shape=jax.ShapeDtypeStruct((K, 16, 1024), BF),...  120 us
    unnamed x4, local copies, waits for them, and re-layouts  4.65 us

profile of v3, /device:TPU:1, one launch (start us, length us, event | category | flops | bytes accessed | tf_op | source)
XLA Modules:
  0.0 124.2 jit_solution(8578317279217099294)
XLA Ops:
  0.0 1.8 %copy.3.l_hbm = bf16[120,8,448]{2,1,0:T(8,128)(2,1)S(1)} copy(bf16[120,8,448]{0,2,1:T(8,128)(2,1)} %param.3) | data formatting | bytes 1720320 | tf_op args[1]
  1.8 0.0 copy-start
  1.9 1.5 %copy-done = bf16[60,2,8,1024]{3,2,1,0:T(8,128)(2,1)S(1)} copy-done((bf16[60,2,8,1024]{3,2,1,0:T(8,128)(2,1)S(1)}, bf16[60,2,8,1024]{3,2,1,0:T(8,128)(2,1)}, u32[]{:S(2)}) %copy-start) | copy-done | bytes 1966104
  3.4 119.5 %shard_map.28 = bf16[60,16,1024]{2,1,0:T(8,128)(2,1)S(1)} custom-call(bf16[60,16,1024]{2,1,0:T(8,128)(2,1)S(1)} %bitcast.3, bf16[120,8,448]{2,1,0:T(8,128)(2,1)S(1)} %copy.3.l_hbm), custom_call_target="tpu_custom_call" | custom-call | tf_op jit(solution)/shard_map/pallas_call | solution.py:243
  122.9 1.3 %copy.5 = bf16[60,2,8,1024]{3,2,1,0:T(8,128)(2,1)} copy(bf16[60,2,8,1024]{3,2,1,0:T(8,128)(2,1)S(1)} %bitcast.2) | data formatting | bytes 3932160
Async XLA Ops:
  1.8 1.5 %copy-start = (bf16[60,2,8,1024]{3,2,1,0:T(8,128)(2,1)S(1)}, bf16[60,2,8,1024]{3,2,1,0:T(8,128)(2,1)}, u32[]{:S(2)}) copy-start(bf16[60,2,8,1024]{3,2,1,0:T(8,128)(2,1)} %param.2) | copy-start | bytes 5898244

commit v4 on v0

v4 whole, which is shorter than its diff:
```python
import jax
import jax.numpy as jnp
from jax import lax
from jax.experimental import pallas as pl
from jax.experimental.pallas import tpu as pltpu
from jax.sharding import PartitionSpec as P

MESH = pl.DeviceIdType.MESH
BF, F32 = jnp.bfloat16, jnp.float32
K, VEC = 60, 448
COLS, DEPTH = 16, 8
CUTS, CUT = 5, 12
SENDERS = COLS + DEPTH
MAIN, EDGE = 384, 128


PEERS, BLOCKS = (COLS, DEPTH), (DEPTH, COLS)


def kernel(t_hbm, l_hbm, out_ref, t_ref, l_ref, slab_a, slab_b, slab_c, edge, edge_in, send, t_in, r_in,
           rs_a, rs_b, rs_c, rb_a, rb_b, rb_c, mine_a, mine_b, mine_c, inter_a, inter_b, inter_c, own_sem, swap_send,
           edge_sem, ring_send, ring_recv, t_send, t_recv, sum_send, sum_recv, share_send, share_recv, r_send, r_recv,
           in_sem):
    load_l = pltpu.make_async_copy(l_hbm, l_ref, in_sem.at[0])
    load_l.start()
    load_t = pltpu.make_async_copy(t_hbm, t_ref, in_sem.at[1])
    load_t.start()
    me, core = lax.axis_index("tile"), lax.axis_index("chol")
    w, z = me // DEPTH, lax.rem(me, DEPTH)
    y, x = w // 4, lax.rem(w, 4)
    slabs, widths = (slab_a, slab_b, slab_c), (MAIN, MAIN, EDGE)
    rss, rbs, mines, inters = (rs_a, rs_b, rs_c), (rb_a, rb_b, rb_c), (mine_a, mine_b, mine_c), (inter_a, inter_b, inter_c)

    def plane(q):
        return lax.rem(y + q // 4, 4) * 4 + lax.rem(x + lax.rem(q, 4), 4)

    def level(d):
        return lax.rem(z + d + DEPTH, DEPTH)

    def near(dx, dy):
        return lax.rem(y + dy + 4, 4) * 4 + lax.rem(x + dx + 4, 4)

    def in_slab(column):
        return lax.rem(column, 2) * 8 + column // 2

    def remote(src, dst, send_sem, recv_sem, tile, to_core):
        return pltpu.make_async_remote_copy(src_ref=src, dst_ref=dst, send_sem=send_sem, recv_sem=recv_sem,
                                            device_id=(tile, to_core), device_id_type=MESH)

    def wait_bytes(ref, sem):
        pltpu.make_async_copy(ref, ref, sem).wait()

    def each(lo, hi, one):
        def step(q, _):
            one(q)
            return 0
        lax.fori_loop(lo, hi, step, 0)

    barrier = pltpu.get_barrier_semaphore()

    def greet(tile, to_core):
        pl.semaphore_signal(barrier, inc=1, device_id=(tile, to_core), device_id_type=MESH)

    @pl.when(core == 0)
    def _():
        each(1, COLS, lambda q: greet(plane(q) * DEPTH + z, 0))
        each(0, COLS, lambda q: greet(plane(q) * DEPTH + z, 1))
        each(1, DEPTH, lambda d: greet(w * DEPTH + level(d), 1))
        for d in (-1, 1):
            greet(w * DEPTH + level(d), 0)
        pl.semaphore_wait(barrier, 2 * COLS + DEPTH)

    @pl.when(core == 1)
    def _():
        each(0, DEPTH, lambda d: greet(w * DEPTH + level(d), 0))
        each(1, DEPTH, lambda d: greet(w * DEPTH + level(d), 1))
        each(1, COLS, lambda q: greet(plane(q) * DEPTH + z, 0))
        for dx, dy in ((1, 0), (-1, 0), (0, 1), (0, -1)):
            greet(near(dx, dy) * DEPTH + z, 1)
        pl.semaphore_wait(barrier, COLS + 2 * DEPTH + 2)

    low = lax.broadcasted_iota(jnp.int32, (16, 128), 1) < 64
    granule = lax.broadcasted_iota(jnp.int32, (16, 128), 1) // 8

    def halves(first, second):
        return (jnp.where(low, first, pltpu.roll(second, 64, 1)), jnp.where(low, pltpu.roll(first, 64, 1), second))

    def swap(blocks):
        for bit in (1, 2, 4):
            take = (granule & bit) != 0
            new = list(blocks)
            for i in range(8):
                if not i & bit:
                    first, second = blocks[i], blocks[i | bit]
                    new[i] = jnp.where(take, pltpu.roll(second, 8 * bit, 1), first)
                    new[i | bit] = jnp.where(take, second, pltpu.roll(first, 128 - 8 * bit, 1))
            blocks = new
        return blocks

    def tile_of(m):
        return pl.ds(pl.multiple_of(m * 128, 128), 128)

    def run(c):
        peers, blocks = PEERS[c], BLOCKS[c]
        wide = CUT * 8 * blocks

        def piece_of(buffer, n, place):
            if c == 0:
                return buffer.at[n, place // 2, :, pl.ds(pl.multiple_of(lax.rem(place, 2) * wide, 128), wide)]
            return buffer.at[n, place]

        own = z if c == 0 else in_slab(w)
        place_in_rows = w if c == 0 else z
        sent = []

        def peer(q):
            return plane(q) if c == 0 else level(q)

        def tile(q):
            return plane(q) * DEPTH + z if c == 0 else w * DEPTH + level(q)

        def vectors(owner, where, sem):
            if c != owner:
                return
            pltpu.make_async_copy(l_hbm.at[pl.ds(c * K, K), :, pl.ds(0, MAIN)], where.at[:, own], sem).start()
            theirs = in_slab(w) if c == 0 else z
            remote(l_hbm.at[pl.ds((1 - c) * K, K), :, pl.ds(0, MAIN)], where.at[:, theirs], swap_send.at[0], sem, me,
                   1 - c).start()

        def pass_on(p, rows, block, n, to):
            piece = slabs[p].at[rows, block]
            copy = remote(piece, piece, ring_send.at[n], ring_recv.at[n], to, c)
            copy.start()
            sent.append(copy)

        def z_ring(p, hop):
            for sub in range(4):
                for way in range(2):
                    if hop == 3 and sub % 2 != way:
                        continue
                    if hop:
                        z_arrived(p, sub, way, hop - 1)
                    pass_on(p, pl.ds(sub * 15, 15), level(-hop if way == 0 else hop), ((p * 4 + sub) * 2 + way) * 4 + hop,
                            w * DEPTH + level(1 if way == 0 else -1))

        def z_arrived(p, sub, way, hop):
            step = -1 - hop if way == 0 else 1 + hop
            wait_bytes(slabs[p].at[pl.ds(sub * 15, 15), level(step)], ring_recv.at[((p * 4 + sub) * 2 + way) * 4 + hop])

        def xy_number(p, half, a, b):
            return (p * 2 + half) * 16 + a % 4 * 4 + b % 4

        def xy_block(half, a, b):
            return in_slab(near(*((a, b) if half == 0 else (b, a))))

        def xy_send(p, half, second, way, a, b):
            to = near(way, 0) if (half == 0) != second else near(0, way)
            n = xy_number(p, half, a, b - way) if second else xy_number(p, half, a - way, b)
            pass_on(p, pl.ds(half * 30, 30), xy_block(half, a, b), n, to * DEPTH + z)

        def xy_arrived(p, half, a, b):
            wait_bytes(slabs[p].at[pl.ds(half * 30, 30), xy_block(half, a, b)], ring_recv.at[xy_number(p, half, a, b)])

        def xy_ring(p, stage):
            for half in range(2):
                if stage == 0:
                    for second in (False, True):
                        for way in (1, -1):
                            xy_send(p, half, second, way, 0, 0)
                if stage == 1:
                    for a in (3, 1):
                        xy_arrived(p, half, a, 0)
                        if a == 3:
                            xy_send(p, half, False, 1, a, 0)
                        for way in (1, -1):
                            xy_send(p, half, True, way, a, 0)
                if stage == 2:
                    xy_arrived(p, half, 0, 3)
                    xy_send(p, half, True, 1, 0, 3)
                    xy_arrived(p, half, 2, 0)
                    for way in (1, -1):
                        xy_send(p, half, True, way, 2, 0)
                if stage == 3:
                    for a in (3, 1):
                        xy_arrived(p, half, a, 1)
                        xy_send(p, half, True, -1, a, 1)
                    xy_arrived(p, half, 2, 3)
                    xy_send(p, half, True, 1, 2, 3)

        def last(p):
            if c == 0:
                for sub in range(4):
                    z_arrived(p, sub, 1 - sub % 2, 2)
                    z_arrived(p, sub, sub % 2, 3)
            else:
                for half in range(2):
                    for a, b in ((0, 1), (3, 3), (1, 3), (2, 1), (0, 2), (3, 2), (1, 2), (2, 2)):
                        xy_arrived(p, half, a, b)

        ring = z_ring if c == 0 else xy_ring

        def shuffle(n):
            if c == 0:
                def lane_tile(m):
                    for pair in range(CUT // 2):
                        k = n * CUT + 2 * pair
                        for side, block in enumerate(halves(t_ref[k, :, tile_of(m)].astype(F32),
                                                            t_ref[k + 1, :, tile_of(m)].astype(F32))):
                            at = side * wide + pair * 128
                            send[n, m, :, at:at + 128] = block.astype(BF)
                each(0, COLS // 2, lane_tile)
            else:
                def one_row(k):
                    for i, block in enumerate(swap([t_ref[n * CUT + k, :, m * 128:(m + 1) * 128].astype(F32)
                                                    for m in range(8)])):
                        send[n, i, :, tile_of(k)] = block.astype(BF)
                each(0, CUT, one_row)

        def unshuffle(n):
            if c == 0:
                def lane_tile(m):
                    for pair in range(CUT // 2):
                        lo, hi, k = pair * 128, wide + pair * 128, n * CUT + 2 * pair
                        for side, block in enumerate(halves(r_in[n, m, :, lo:lo + 128].astype(F32),
                                                            r_in[n, m, :, hi:hi + 128].astype(F32))):
                            out_ref[k + side, :, tile_of(m)] = block.astype(BF)
                each(0, COLS // 2, lane_tile)
            else:
                def one_row(k):
                    for m, block in enumerate(swap([r_in[n, i, :, tile_of(k)].astype(F32) for i in range(8)])):
                        out_ref[n * CUT + k, :, m * 128:(m + 1) * 128] = block.astype(BF)
                each(0, CUT, one_row)

        def exchange(n, into, send_sem, recv_sem):
            here = place_in_rows
            pltpu.make_async_copy(piece_of(send, n, here), piece_of(into, n, here), recv_sem.at[n]).start()
            each(1, peers, lambda q: remote(piece_of(send, n, peer(q)), piece_of(into, n, here), send_sem.at[n],
                                            recv_sem.at[n], tile(q), c).start())

        def all_but_one(n):
            if c == 0:
                return t_ref.at[pl.ds(0, COLS - 1), :, pl.ds(0, wide)]
            return t_in.at[n, pl.ds(0, DEPTH - 1)]

        def vectors_of(p, n):
            return slabs[p][n * CUT:(n + 1) * CUT, :blocks].reshape(wide, widths[p])

        def multiply1(p):
            total = None
            for n in range(CUTS):
                if c == 0:
                    rows = jnp.concatenate([t_in[n, :, :, :wide].reshape(128, wide), t_in[n, :, :, wide:].reshape(128, wide)])
                else:
                    rows = t_in[n].reshape(128, wide)
                term = jnp.dot(rows, vectors_of(p, n), preferred_element_type=F32)
                total = term if total is None else total + term
            rss[p][:peers] = total.astype(BF).reshape(peers, 2, 8, widths[p])

        def sums_of(place):
            return in_slab(place) if c == 0 else place

        def add_up(p):
            first = 0 if c == 0 else COLS
            pltpu.make_async_copy(rss[p].at[sums_of(place_in_rows), c], rbs[p].at[first], sum_recv.at[p]).start()

            def one(q):
                n, to_core = q // 2, lax.rem(q + c, 2)
                remote(rss[p].at[sums_of(peer(n)), to_core], rbs[p].at[first + n], sum_send.at[p], sum_recv.at[p], tile(n),
                       to_core).start()
            each(1, 2 * peers, one)

        def share(p):
            wait_bytes(rbs[p].at[pl.ds(0, SENDERS)], sum_recv.at[p])
            total = rbs[p][0].astype(F32)
            for n in range(1, SENDERS):
                total = total + rbs[p][n].astype(F32)
            mines[p][...] = total.astype(BF)
            pltpu.make_async_copy(mines[p], inters[p].at[place_in_rows, c], share_recv.at[p]).start()
            each(1 if c == 0 else 0, COLS, lambda q: remote(
                mines[p], inters[p].at[w, c], share_send.at[p], share_recv.at[p], plane(q) * DEPTH + z, 0).start())
            each(1 if c == 1 else 0, DEPTH, lambda d: remote(
                mines[p], inters[p].at[z, c], share_send.at[p], share_recv.at[p], w * DEPTH + level(d), 1).start())

        def multiply2(n):
            total = None
            for p in range(3):
                rows = inters[p][:peers].reshape(peers * 16, widths[p])
                term = lax.dot_general(rows, vectors_of(p, n), (((1,), (1,)), ((), ())), preferred_element_type=F32)
                total = term if total is None else total + term
            if c == 0:
                total = total.astype(BF).reshape(8, 2, 16, wide)
                send[n, :, :, :wide] = total[:, 0]
                send[n, :, :, wide:] = total[:, 1]
            else:
                send[n] = total.astype(BF).reshape(8, 16, wide)

        vectors(0, slab_a, own_sem.at[0])
        vectors(1, slab_b, own_sem.at[1])
        wait_bytes(slab_a.at[:, own], own_sem.at[0])
        ring(0, 0)
        load_l.wait()
        row = lax.broadcasted_iota(jnp.int32, (VEC - MAIN, EDGE), 0)
        column = lax.broadcasted_iota(jnp.int32, (VEC - MAIN, EDGE), 1)
        place = (column == row + (VEC - MAIN) * c).astype(BF)
        tail = jnp.dot(l_ref[:, :, MAIN:].reshape(2 * K * 8, VEC - MAIN), place, preferred_element_type=F32)
        edge[...] = tail.astype(BF).reshape(2 * K, 8, EDGE)
        to_sibling = remote(edge.at[pl.ds((1 - c) * K, K)], edge_in, edge_sem.at[0], edge_sem.at[1], me, 1 - c)
        to_sibling.start()
        load_t.wait()
        for n in range(CUTS):
            shuffle(n)
            exchange(n, t_in, t_send, t_recv)
        to_sibling.wait_recv()

        def merge(k):
            slab_c[k, own] = (edge[c * K + k].astype(F32) + edge_in[k].astype(F32)).astype(BF)
        each(0, K, merge)
        for stage in (1, 2, 3):
            ring(0, stage)
        wait_bytes(slab_b.at[:, own], own_sem.at[1])
        ring(1, 0)
        ring(2, 0)
        last(0)
        for n in range(CUTS):
            wait_bytes(t_in.at[n], t_recv.at[n])
        multiply1(0)
        add_up(0)
        ring(1, 1)
        ring(2, 1)
        share(0)
        for stage in (2, 3):
            ring(1, stage)
            ring(2, stage)
        for n in range(CUTS):
            wait_bytes(all_but_one(n), t_send.at[n])
        last(1)
        multiply1(1)
        add_up(1)
        last(2)
        multiply1(2)
        add_up(2)
        share(1)
        share(2)
        for p in range(3):
            wait_bytes(inters[p].at[pl.ds(0, peers)], share_recv.at[p])
        for n in range(CUTS):
            multiply2(n)
            exchange(n, r_in, r_send, r_recv)
        for n in range(CUTS):
            wait_bytes(r_in.at[n], r_recv.at[n])
            unshuffle(n)

        for copy in sent + [to_sibling]:
            copy.wait_send()
        wait_bytes(slabs[c].at[:, own], swap_send.at[0])
        for n in range(CUTS):
            wait_bytes(all_but_one(n), r_send.at[n])
        for p in range(3):
            wait_bytes(rbs[p].at[pl.ds(0, 2 * peers - 1)], sum_send.at[p])
            wait_bytes(rbs[p].at[pl.ds(0, SENDERS - 1)], share_send.at[p])

    pl.when(core == 0)(lambda: run(0))
    pl.when(core == 1)(lambda: run(1))


def shards(amplitudes, cholesky):
    dma, V = pltpu.SemaphoreType.DMA, pltpu.VMEM
    widths = (MAIN, MAIN, EDGE)
    out = pl.pallas_call(
        kernel,
        out_shape=jax.ShapeDtypeStruct((K, 16, 1024), BF),
        in_specs=[pl.BlockSpec(memory_space=pl.ANY)] * 2,
        out_specs=pl.BlockSpec(memory_space=pltpu.VMEM),
        scratch_shapes=[
            V((K, 16, 1024), BF), V((2 * K, 8, VEC), BF),
            *[V((K, COLS, 8, n), BF) for n in widths],
            V((2 * K, 8, EDGE), BF), V((K, 8, EDGE), BF),
            *[V((CUTS, DEPTH, 16, CUT * 8 * COLS), BF)] * 3,
            *[V((COLS, 2, 8, n), BF) for n in widths], *[V((2 * COLS, 8, n), BF) for n in widths],
            *[V((8, n), BF) for n in widths], *[V((COLS, 2, 8, n), BF) for n in widths],
            dma((2,)), dma((1,)), dma((2,)), dma((96,)), dma((96,)), dma((CUTS,)), dma((CUTS,)),
            dma((3,)), dma((3,)), dma((3,)), dma((3,)), dma((CUTS,)), dma((CUTS,)), dma((2,)),
        ],
        compiler_params=pltpu.CompilerParams(has_side_effects=True, collective_id=0, vmem_limit_bytes=44 * 2**20),
    )(amplitudes.reshape(K, 16, 1024), cholesky)
    return out.reshape(amplitudes.shape)


def solution(mesh):
    in_specs = (P("chol", None, "tile", None), P(None, "tile", "chol"))
    out_specs = P("chol", None, "tile", None)
    return jax.shard_map(shards, mesh=mesh, in_specs=in_specs, out_specs=out_specs, check_vma=False)
```

time: 505 us -> 118 us (0.23)
  blocking collectives: 199 us -> 0 us
  waiting for transfers between devices: 152 us -> 0 us
  Pallas kernels: 0 us -> 114 us
  local copies, waits for them, and re-layouts: 114 us -> 4.65 us
  starting transfers between devices: 16.6 us -> 0 us
  between operations: 13.5 us -> 0.03 us
  matrix products: 9.4 us -> 0 us
    unnamed x1 -> x0, blocking collectives: 138 us -> none
    all_gather x2 -> x0, waiting for transfers between devices: 130 us -> none  [the longest x1 111 us: shards(): lax.all_gather(shared_rows, ('tile', 'chol'), axis=0, tiled=True)]
    pallas_call x0 -> x1, Pallas kernels: none -> 114 us  [shards(): pl.pallas_call(kernel, out_shape=jax.ShapeDtypeStruct((K, 16, 1024), BF),...]
    unnamed x9 -> x4, local copies, waits for them, and re-layouts: 72 us -> 4.65 us
    all_to_all x1 -> x0, blocking collectives: 60.2 us -> none  [shards(): lax.all_to_all(local_cycle, 'tile', split_axis=2, concat_axis=3, tiled=True)]
    all_to_all x4 -> x0, local copies, waits for them, and re-layouts: 22.9 us -> none  [the longest x2 11.8 us: shards(): lax.all_to_all(amplitudes, 'tile', split_axis=3, concat_axis=2, tiled=True)]
    all_to_all x1 -> x0, waiting for transfers between devices: 22.7 us -> none  [shards(): lax.all_to_all(amplitudes, 'tile', split_axis=3, concat_axis=2, tiled=True)]
    all_to_all x1 -> x0, starting transfers between devices: 16.3 us -> none  [shards(): lax.all_to_all(amplitudes, 'tile', split_axis=3, concat_axis=2, tiled=True)]
  transfers between devices with their start and end apart: 3 -> 0, of which waited for: 3 -> 0; matrix products, arithmetic and copies ran while one was open for 2% -> 0% of each run, Pallas kernels for 0% -> 0%
where the time goes in v4:
time: 118 us
  Pallas kernels  114 us (97%)
  local copies, waits for them, and re-layouts  4.65 us (4%)
    pallas_call x1, Pallas kernels, shards(): pl.pallas_call(kernel, out_shape=jax.ShapeDtypeStruct((K, 16, 1024), BF),...  114 us
    unnamed x4, local copies, waits for them, and re-layouts  4.65 us

profile of v4, /device:TPU:1, one launch (start us, length us, event | category | flops | bytes accessed | tf_op | source)
XLA Modules:
  0.0 118.3 jit_solution(1766243817638776307)
XLA Ops:
  0.0 1.8 %copy.3.l_hbm = bf16[120,8,448]{2,1,0:T(8,128)(2,1)S(1)} copy(bf16[120,8,448]{0,2,1:T(8,128)(2,1)} %param.3) | data formatting | bytes 1720320 | tf_op args[1]
  1.8 0.0 copy-start
  1.9 1.5 %copy-done = bf16[60,2,8,1024]{3,2,1,0:T(8,128)(2,1)S(1)} copy-done((bf16[60,2,8,1024]{3,2,1,0:T(8,128)(2,1)S(1)}, bf16[60,2,8,1024]{3,2,1,0:T(8,128)(2,1)}, u32[]{:S(2)}) %copy-start) | copy-done | bytes 1966104
  3.4 113.6 %shard_map.28 = bf16[60,16,1024]{2,1,0:T(8,128)(2,1)S(1)} custom-call(bf16[60,16,1024]{2,1,0:T(8,128)(2,1)S(1)} %bitcast.3, bf16[120,8,448]{2,1,0:T(8,128)(2,1)S(1)} %copy.3.l_hbm), custom_call_target="tpu_custom_call" | custom-call | tf_op jit(solution)/shard_map/pallas_call | solution.py:369
  117.0 1.3 %copy.5 = bf16[60,2,8,1024]{3,2,1,0:T(8,128)(2,1)} copy(bf16[60,2,8,1024]{3,2,1,0:T(8,128)(2,1)S(1)} %bitcast.2) | data formatting | bytes 3932160
Async XLA Ops:
  1.8 1.5 %copy-start = (bf16[60,2,8,1024]{3,2,1,0:T(8,128)(2,1)S(1)}, bf16[60,2,8,1024]{3,2,1,0:T(8,128)(2,1)}, u32[]{:S(2)}) copy-start(bf16[60,2,8,1024]{3,2,1,0:T(8,128)(2,1)} %param.2) | copy-start | bytes 5898244

commit v5 on v4

--- a/solution.py
+++ b/solution.py
@@ -9,7 +9,7 @@
 BF, F32 = jnp.bfloat16, jnp.float32
 K, VEC = 60, 448
 COLS, DEPTH = 16, 8
-CUTS, CUT = 5, 12
+CUTS, CUT = 10, 6
 SENDERS = COLS + DEPTH
 MAIN, EDGE = 384, 128
 
@@ -204,16 +204,16 @@
                 def lane_tile(m):
                     for pair in range(CUT // 2):
                         k = n * CUT + 2 * pair
-                        for side, block in enumerate(halves(t_ref[k, :, tile_of(m)].astype(F32),
-                                                            t_ref[k + 1, :, tile_of(m)].astype(F32))):
+                        for side, block in enumerate(halves(t_ref[k, :, tile_of(m)],
+                                                            t_ref[k + 1, :, tile_of(m)])):
                             at = side * wide + pair * 128
-                            send[n, m, :, at:at + 128] = block.astype(BF)
+                            send[n, m, :, at:at + 128] = block
                 each(0, COLS // 2, lane_tile)
             else:
                 def one_row(k):
-                    for i, block in enumerate(swap([t_ref[n * CUT + k, :, m * 128:(m + 1) * 128].astype(F32)
+                    for i, block in enumerate(swap([t_ref[n * CUT + k, :, m * 128:(m + 1) * 128]
                                                     for m in range(8)])):
-                        send[n, i, :, tile_of(k)] = block.astype(BF)
+                        send[n, i, :, tile_of(k)] = block
                 each(0, CUT, one_row)
 
         def unshuffle(n):
@@ -221,14 +221,14 @@
                 def lane_tile(m):
                     for pair in range(CUT // 2):
                         lo, hi, k = pair * 128, wide + pair * 128, n * CUT + 2 * pair
-                        for side, block in enumerate(halves(r_in[n, m, :, lo:lo + 128].astype(F32),
-                                                            r_in[n, m, :, hi:hi + 128].astype(F32))):
-                            out_ref[k + side, :, tile_of(m)] = block.astype(BF)
+                        for side, block in enumerate(halves(r_in[n, m, :, lo:lo + 128],
+                                                            r_in[n, m, :, hi:hi + 128])):
+                            out_ref[k + side, :, tile_of(m)] = block
                 each(0, COLS // 2, lane_tile)
             else:
                 def one_row(k):
-                    for m, block in enumerate(swap([r_in[n, i, :, tile_of(k)].astype(F32) for i in range(8)])):
-                        out_ref[n * CUT + k, :, m * 128:(m + 1) * 128] = block.astype(BF)
+                    for m, block in enumerate(swap([r_in[n, i, :, tile_of(k)] for i in range(8)])):
+                        out_ref[n * CUT + k, :, m * 128:(m + 1) * 128] = block
                 each(0, CUT, one_row)
 
         def exchange(n, into, send_sem, recv_sem):
@@ -307,30 +307,37 @@
         to_sibling = remote(edge.at[pl.ds((1 - c) * K, K)], edge_in, edge_sem.at[0], edge_sem.at[1], me, 1 - c)
         to_sibling.start()
         load_t.wait()
-        for n in range(CUTS):
-            shuffle(n)
-            exchange(n, t_in, t_send, t_recv)
+
+        def deal(*cuts):
+            for n in cuts:
+                shuffle(n)
+                exchange(n, t_in, t_send, t_recv)
+        deal(0, 1, 2, 3)
+        ring(0, 1)
+        deal(4, 5, 6, 7)
+        ring(0, 2)
+        deal(8, 9)
+        ring(0, 3)
         to_sibling.wait_recv()
 
         def merge(k):
             slab_c[k, own] = (edge[c * K + k].astype(F32) + edge_in[k].astype(F32)).astype(BF)
         each(0, K, merge)
-        for stage in (1, 2, 3):
-            ring(0, stage)
         wait_bytes(slab_b.at[:, own], own_sem.at[1])
         ring(1, 0)
         ring(2, 0)
+        ring(1, 1)
+        ring(2, 1)
         last(0)
         for n in range(CUTS):
             wait_bytes(t_in.at[n], t_recv.at[n])
         multiply1(0)
         add_up(0)
-        ring(1, 1)
-        ring(2, 1)
+        ring(1, 2)
+        ring(2, 2)
         share(0)
-        for stage in (2, 3):
-            ring(1, stage)
-            ring(2, stage)
+        ring(1, 3)
+        ring(2, 3)
         for n in range(CUTS):
             wait_bytes(all_but_one(n), t_send.at[n])
         last(1)

time: 118 us -> 117 us (level)
  no operation moved by 1% of the time
where the time goes in v5:
time: 117 us
  Pallas kernels  113 us (97%)
  local copies, waits for them, and re-layouts  4.65 us (4%)
    pallas_call x1, Pallas kernels, shards(): pl.pallas_call(kernel, out_shape=jax.ShapeDtypeStruct((K, 16, 1024), BF),...  113 us
    unnamed x4, local copies, waits for them, and re-layouts  4.65 us

profile of v5, /device:TPU:1, one launch (start us, length us, event | category | flops | bytes accessed | tf_op | source)
XLA Modules:
  0.0 117.3 jit_solution(107056575429142853)
XLA Ops:
  0.0 1.8 %copy.3.l_hbm = bf16[120,8,448]{2,1,0:T(8,128)(2,1)S(1)} copy(bf16[120,8,448]{0,2,1:T(8,128)(2,1)} %param.3) | data formatting | bytes 1720320 | tf_op args[1]
  1.8 0.0 copy-start
  1.9 1.5 %copy-done = bf16[60,2,8,1024]{3,2,1,0:T(8,128)(2,1)S(1)} copy-done((bf16[60,2,8,1024]{3,2,1,0:T(8,128)(2,1)S(1)}, bf16[60,2,8,1024]{3,2,1,0:T(8,128)(2,1)}, u32[]{:S(2)}) %copy-start) | copy-done | bytes 1966104
  3.4 112.6 %shard_map.28 = bf16[60,16,1024]{2,1,0:T(8,128)(2,1)S(1)} custom-call(bf16[60,16,1024]{2,1,0:T(8,128)(2,1)S(1)} %bitcast.3, bf16[120,8,448]{2,1,0:T(8,128)(2,1)S(1)} %copy.3.l_hbm), custom_call_target="tpu_custom_call" | custom-call | tf_op jit(solution)/shard_map/pallas_call | solution.py:376
  116.0 1.3 %copy.5 = bf16[60,2,8,1024]{3,2,1,0:T(8,128)(2,1)} copy(bf16[60,2,8,1024]{3,2,1,0:T(8,128)(2,1)S(1)} %bitcast.2) | data formatting | bytes 3932160
Async XLA Ops:
  1.8 1.5 %copy-start = (bf16[60,2,8,1024]{3,2,1,0:T(8,128)(2,1)S(1)}, bf16[60,2,8,1024]{3,2,1,0:T(8,128)(2,1)}, u32[]{:S(2)}) copy-start(bf16[60,2,8,1024]{3,2,1,0:T(8,128)(2,1)} %param.2) | copy-start | bytes 5898244

commit v6 on v5

--- a/solution.py
+++ b/solution.py
@@ -32,7 +32,7 @@
     rss, rbs, mines, inters = (rs_a, rs_b, rs_c), (rb_a, rb_b, rb_c), (mine_a, mine_b, mine_c), (inter_a, inter_b, inter_c)
 
     def plane(q):
-        return lax.rem(y + q // 4, 4) * 4 + lax.rem(x + lax.rem(q, 4), 4)
+        return lax.rem(y + q // 4, 4) * 4 + lax.rem(x + q % 4, 4)
 
     def level(d):
         return lax.rem(z + d + DEPTH, DEPTH)
@@ -264,10 +264,11 @@
             pltpu.make_async_copy(rss[p].at[sums_of(place_in_rows), c], rbs[p].at[first], sum_recv.at[p]).start()
 
             def one(q):
-                n, to_core = q // 2, lax.rem(q + c, 2)
+                n, to_core = q // 2, (q + c) % 2
                 remote(rss[p].at[sums_of(peer(n)), to_core], rbs[p].at[first + n], sum_send.at[p], sum_recv.at[p], tile(n),
                        to_core).start()
-            each(1, 2 * peers, one)
+            for q in range(1, 2 * peers):
+                one(q)
 
         def share(p):
             wait_bytes(rbs[p].at[pl.ds(0, SENDERS)], sum_recv.at[p])
@@ -276,10 +277,10 @@
                 total = total + rbs[p][n].astype(F32)
             mines[p][...] = total.astype(BF)
             pltpu.make_async_copy(mines[p], inters[p].at[place_in_rows, c], share_recv.at[p]).start()
-            each(1 if c == 0 else 0, COLS, lambda q: remote(
-                mines[p], inters[p].at[w, c], share_send.at[p], share_recv.at[p], plane(q) * DEPTH + z, 0).start())
-            each(1 if c == 1 else 0, DEPTH, lambda d: remote(
-                mines[p], inters[p].at[z, c], share_send.at[p], share_recv.at[p], w * DEPTH + level(d), 1).start())
+            for q in range(1 if c == 0 else 0, COLS):
+                remote(mines[p], inters[p].at[w, c], share_send.at[p], share_recv.at[p], plane(q) * DEPTH + z, 0).start()
+            for d in range(1 if c == 1 else 0, DEPTH):
+                remote(mines[p], inters[p].at[z, c], share_send.at[p], share_recv.at[p], w * DEPTH + level(d), 1).start()
 
         def multiply2(n):
             total = None

time: 117 us -> 117 us (level)
  no operation moved by 1% of the time
where the time goes in v6:
time: 117 us
  Pallas kernels  112 us (96%)
  local copies, waits for them, and re-layouts  4.65 us (4%)
    pallas_call x1, Pallas kernels, shards(): pl.pallas_call(kernel, out_shape=jax.ShapeDtypeStruct((K, 16, 1024), BF),...  112 us
    unnamed x4, local copies, waits for them, and re-layouts  4.65 us

profile of v6, /device:TPU:1, one launch (start us, length us, event | category | flops | bytes accessed | tf_op | source)
XLA Modules:
  0.0 116.7 jit_solution(14433997482632856265)
XLA Ops:
  0.0 1.8 %copy.3.l_hbm = bf16[120,8,448]{2,1,0:T(8,128)(2,1)S(1)} copy(bf16[120,8,448]{0,2,1:T(8,128)(2,1)} %param.3) | data formatting | bytes 1720320 | tf_op args[1]
  1.8 0.0 copy-start
  1.9 1.5 %copy-done = bf16[60,2,8,1024]{3,2,1,0:T(8,128)(2,1)S(1)} copy-done((bf16[60,2,8,1024]{3,2,1,0:T(8,128)(2,1)S(1)}, bf16[60,2,8,1024]{3,2,1,0:T(8,128)(2,1)}, u32[]{:S(2)}) %copy-start) | copy-done | bytes 1966104
  3.4 112.0 %shard_map.28 = bf16[60,16,1024]{2,1,0:T(8,128)(2,1)S(1)} custom-call(bf16[60,16,1024]{2,1,0:T(8,128)(2,1)S(1)} %bitcast.3, bf16[120,8,448]{2,1,0:T(8,128)(2,1)S(1)} %copy.3.l_hbm), custom_call_target="tpu_custom_call" | custom-call | tf_op jit(solution)/shard_map/pallas_call | solution.py:377
  115.4 1.3 %copy.5 = bf16[60,2,8,1024]{3,2,1,0:T(8,128)(2,1)} copy(bf16[60,2,8,1024]{3,2,1,0:T(8,128)(2,1)S(1)} %bitcast.2) | data formatting | bytes 3932160
Async XLA Ops:
  1.8 1.5 %copy-start = (bf16[60,2,8,1024]{3,2,1,0:T(8,128)(2,1)S(1)}, bf16[60,2,8,1024]{3,2,1,0:T(8,128)(2,1)}, u32[]{:S(2)}) copy-start(bf16[60,2,8,1024]{3,2,1,0:T(8,128)(2,1)} %param.2) | copy-start | bytes 5898244
